TPU v7x, 32 devices: a whole 2x2x4 slice. The times are simulated.
32 devices in a mesh: blk: 8 (over z, x), xor: 4 (over y, core).
Axes of the slice: x: 2, y: 2, z: 4, core: 2. Of those that a mesh axis runs over, the one named last changes fastest.
Arguments:
- users: float32 [32768, 256], P(('blk', 'xor')), may hold values from -1.5 to 1.5
- user_accum: float32 [32768, 256], P(('blk', 'xor')), may hold values from 0.05 to 1
- items: float32 [16384, 256], P(('blk', 'xor')), may hold values from -1.5 to 1.5
- item_accum: float32 [16384, 256], P(('blk', 'xor')), may hold values from 0.05 to 1
- seen_user: int32 [6, 512], P(None, ('blk', 'xor')), may hold values from 0 to 7
- seen_item: int32 [6, 512], P(None, ('blk', 'xor')), may hold values from 0 to 3
- row_live: int32 [6, 512, 128], P(None, ('blk', 'xor')), may hold values 0 or 1
- col_live: int32 [6, 512, 128], P(None, ('blk', 'xor')), may hold values 0 or 1
- neg_user: int32 [6, 256], P(None, ('blk', 'xor')), may hold values from 0 to 7
- neg_item: int32 [6, 256], P(None, ('blk', 'xor')), may hold values from 0 to 3
Outputs:
- users_out: float32 [32768, 256], P(('blk', 'xor'))
- user_accum_out: float32 [32768, 256], P(('blk', 'xor'))
- items_out: float32 [16384, 256], P(('blk', 'xor'))
- item_accum_out: float32 [16384, 256], P(('blk', 'xor'))
All inputs are finite; a program needn't handle non-finite values. No bound on the sum of `row_live` or of `col_live` on one device may be relied on, other than what follows from the above.
Results may differ from a plain program's by a relative error of at most 0.0051.
Values sent between devices are 32-bit elements; how exact they have to be, the bound alone decides.
A program may use at most 64 MiB of HBM per device.

v0:
```python
import functools

import jax
import jax.numpy as jnp
from jax import lax
from jax.experimental import pallas as pl
from jax.experimental.pallas import tpu as pltpu
from jax.sharding import PartitionSpec as P

SUBS = 6
TILE = 128
LEARN_RATE = 0.05
DECAY = 0.02
NEG_WEIGHT = 0.25
MESH = pl.DeviceIdType.MESH
F32 = jnp.float32
BF16 = jnp.bfloat16


def flipped(index, bit):
    step = 2**bit
    return index + step - 2 * step * ((index // step) % 2)


def as_column(row):
    n = row.shape[1]
    full = jnp.broadcast_to(row, (n, n))
    diagonal = lax.broadcasted_iota(jnp.int32, (n, n), 0) == lax.broadcasted_iota(
        jnp.int32, (n, n), 1
    )
    return jnp.sum(jnp.where(diagonal, full, 0), axis=1, keepdims=True)


def one_hot_rows(column, live, tiles):
    return jnp.concatenate(
        [jnp.where(column == tile, live, 0.0) for tile in range(tiles)], axis=1
    )


def dot(a, b, ca, cb):
    return lax.dot_general(a, b, (((ca,), (cb,)), ((), ())), preferred_element_type=F32)


def kernel(
    n_blk,
    users_ref,
    user_accum_ref,
    items_ref,
    item_accum_ref,
    seen_user_ref,
    seen_item_ref,
    row_live_ref,
    col_live_ref,
    neg_user_ref,
    neg_item_ref,
    users_out,
    user_accum_out,
    items_out,
    item_accum_out,
    state,
    ub,
    vb,
    grad_users,
    grad_items,
    rows,
    cols,
    send_sem,
    recv_sem,
):
    blk = lax.axis_index("blk")
    xor = lax.axis_index("xor")
    ahead = lax.rem(blk + 1, n_blk)
    behind = lax.rem(blk + n_blk - 1, n_blk)

    barrier = pltpu.get_barrier_semaphore()
    for other in (xor, flipped(xor, 0), flipped(xor, 1)):
        pl.semaphore_signal(barrier, inc=1, device_id=(behind, other), device_id_type=MESH)

    n_users, width = users_ref.shape
    half = items_ref.shape[0] // 2
    block = 256
    n_obs = seen_user_ref.shape[1]
    n_neg = neg_user_ref.shape[1]
    pad = rows.shape[0] - n_obs - n_neg

    ub[...] = users_ref[...].astype(BF16)

    def masks(s):
        user_tiles, item_tiles = n_users // TILE, 2 * half // TILE
        root = jnp.full((n_neg, TILE), NEG_WEIGHT**0.5, F32)
        for index, negative, live, out, tiles in (
            (seen_user_ref, neg_user_ref, row_live_ref, rows, user_tiles),
            (seen_item_ref, neg_item_ref, col_live_ref, cols, item_tiles),
        ):
            observed = one_hot_rows(
                as_column(index[pl.ds(s, 1), :]), live[s].astype(F32), tiles
            )
            sampled = one_hot_rows(as_column(negative[pl.ds(s, 1), :]), root, tiles)
            out[...] = jnp.concatenate(
                [observed, sampled, jnp.zeros((pad, tiles * TILE), F32)], axis=0
            ).astype(BF16)

    def copy(s, h):
        to = xor if h == 0 else flipped(xor, s % 2)
        return pltpu.make_async_remote_copy(
            src_ref=state.at[s, h],
            dst_ref=state.at[s + 1, h],
            send_sem=send_sem.at[s, h],
            recv_sem=recv_sem.at[s, h],
            device_id=(ahead, to),
            device_id_type=MESH,
        )

    for s in range(SUBS):
        masks(s)
        for h in range(2):
            if s > 0:
                copy(s - 1, h).wait_recv()
            here = pl.ds(h * half, half)
            if s == 0:
                factor, accum = items_ref.at[here], item_accum_ref.at[here]
            else:
                factor, accum = state.at[s, h, 0], state.at[s, h, 1]
            if s == SUBS - 1:
                new_factor, new_accum = items_out.at[here], item_accum_out.at[here]
            else:
                new_factor, new_accum = state.at[s, h, 0], state.at[s, h, 1]
            vb[...] = factor[...].astype(BF16)
            grad_items[...] = DECAY * factor[...]

            def terms(u, carry, h=h):
                span = pl.ds(pl.multiple_of(u * block, block), block)
                here = pl.ds(h * half, half)
                scores = dot(ub[span], vb[...], 1, 1)
                weight = dot(rows[:, span], cols[:, here], 0, 0)
                seen = dot(rows[:n_obs, span], cols[:n_obs, here], 0, 0)
                err = (weight * scores - seen).astype(BF16)
                user_terms = dot(err, vb[...], 1, 0)
                if h == 0:
                    grad_users[span] = user_terms
                else:
                    grad_users[span] += user_terms
                grad_items[...] += dot(err, ub[span], 0, 0)
                return carry

            lax.fori_loop(0, n_users // block, terms, 0)

            grad = grad_items[...]
            summed = accum[...] + grad * grad
            new_accum[...] = summed
            new_factor[...] = factor[...] - LEARN_RATE * grad * lax.rsqrt(summed)
            if s < SUBS - 1:
                if s == 0 and h == 0:
                    pl.semaphore_wait(barrier, 3)
                copy(s, h).start()

        old, old_accum = (
            (users_ref, user_accum_ref) if s == 0 else (users_out, user_accum_out)
        )

        def update(u, carry, old=old, old_accum=old_accum):
            span = pl.ds(pl.multiple_of(u * block, block), block)
            now = old[span]
            grad = grad_users[span] + DECAY * now
            summed = old_accum[span] + grad * grad
            user_accum_out[span] = summed
            now = now - LEARN_RATE * grad * lax.rsqrt(summed)
            users_out[span] = now
            ub[span] = now.astype(BF16)
            return carry

        lax.fori_loop(0, n_users // block, update, 0)

    for s in range(SUBS - 1):
        for h in range(2):
            copy(s, h).wait_send()


def per_device(n_blk, *args):
    users, _, items = args[:3]
    n_users, width = users.shape
    n_items = items.shape[0]
    half = n_items // 2
    entries = -(-(args[4].shape[1] + args[8].shape[1]) // 16) * 16
    vmem = pl.BlockSpec(memory_space=pltpu.VMEM)
    flops = SUBS * 2 * 3 * n_users * n_items * width
    return pl.pallas_call(
        functools.partial(kernel, n_blk),
        out_shape=(
            jax.ShapeDtypeStruct(users.shape, F32),
            jax.ShapeDtypeStruct(users.shape, F32),
            jax.ShapeDtypeStruct(items.shape, F32),
            jax.ShapeDtypeStruct(items.shape, F32),
        ),
        in_specs=[vmem] * 10,
        out_specs=(vmem,) * 4,
        scratch_shapes=[
            pltpu.VMEM((SUBS, 2, 2, half, width), F32),
            pltpu.VMEM((n_users, width), BF16),
            pltpu.VMEM((half, width), BF16),
            pltpu.VMEM((n_users, width), F32),
            pltpu.VMEM((half, width), F32),
            pltpu.VMEM((entries, n_users), BF16),
            pltpu.VMEM((entries, n_items), BF16),
            pltpu.SemaphoreType.DMA((SUBS - 1, 2)),
            pltpu.SemaphoreType.DMA((SUBS - 1, 2)),
        ],
        compiler_params=pltpu.CompilerParams(
            collective_id=0, has_side_effects=True, vmem_limit_bytes=40 * 2**20
        ),
        cost_estimate=pl.CostEstimate(
            flops=flops, bytes_accessed=12 * 2**20, transcendentals=0
        ),
    )(*args)


def solution(mesh):
    flat = P(("blk", "xor"), None)
    tiles = P(None, ("blk", "xor"))
    live = P(None, ("blk", "xor"), None)
    return jax.shard_map(
        functools.partial(per_device, mesh.shape["blk"]),
        mesh=mesh,
        in_specs=(flat, flat, flat, flat, tiles, tiles, live, live, tiles, tiles),
        out_specs=(flat, flat, flat, flat),
        check_vma=False,
    )
```

profile of v0, /device:TPU:1, one launch (start us, length us, event | category | flops | bytes accessed | tf_op | source)
XLA Modules:
  0.0 136.8 jit_solution(2346893071411284208)
XLA Ops:
  0.6 0.0 copy-start
  0.6 1.2 copy-done
  1.9 0.0 copy-start.1
  1.9 1.2 copy-done.1
  3.1 0.0 copy-start.2
  3.1 1.0 copy-done.2
  4.1 0.0 copy-start.3
  4.1 1.0 copy-done.3
  5.2 0.0 copy-start.4
  5.2 0.8 copy-done.4
  6.0 0.0 copy-start.5
  6.0 0.8 copy-done.5
  6.8 0.0 copy-start.6
  6.8 0.7 copy-done.6
  7.5 0.0 copy-start.7
  7.5 0.7 copy-done.7
  8.1 0.0 copy-start.8
  8.1 0.7 copy-done.8
  8.8 0.0 copy-start.9
  8.8 0.7 copy-done.9
  9.5 123.7 %shard_map.129 = (f32[1024,256]{1,0:T(8,128)S(1)}, f32[1024,256]{1,0:T(8,128)S(1)}, f32[512,256]{1,0:T(8,128)S(1)}, f32[512,256]{1,0:T(8,128)S(1)}) custom-call(f32[1024,256]{1,0:T(8,128)S(1)} %copy-done, f32[1024,256]{1,0:T(8,128)S(1)} %copy-done.1, f32[512,256]{1,0:T(8,128)S(1)} %copy-done.2, f32[512,256]{1,0:T(8,128)S(1)} %copy-done.3, ...), custom_call_target="tpu_custom_call" | custom-call | flops 4831838208 | bytes 12582912 | tf_op jit(solution)/shard_map/pallas_call | solution.py:187
  133.3 1.0 copy.18
  134.2 1.0 copy.19
  135.2 0.8 copy.20
  136.0 0.8 copy.21
Async XLA Ops:
  0.6 1.2 copy-start
  1.9 1.2 copy-start.1
  3.1 1.0 copy-start.2
  4.1 1.0 copy-start.3
  5.2 0.8 copy-start.4
  6.0 0.8 copy-start.5
  6.8 0.7 copy-start.6
  7.5 0.7 copy-start.7
  8.1 0.7 copy-start.8
  8.8 0.7 copy-start.9
where the time goes:
time: 137 us
  Pallas kernels  124 us (91%)
  local copies, waits for them, and re-layouts  12.4 us (9%)
    pallas_call x1, Pallas kernels, per_device(): pl.pallas_call(functools.partial(kernel, n_blk), out_shape=(jax.ShapeDtyp...  124 us
    unnamed x24, local copies, waits for them, and re-layouts  12.4 us

commit v1 on v0

v1 whole, which is shorter than its diff:
```python
import functools

import jax
import jax.numpy as jnp
from jax import lax
from jax.experimental import pallas as pl
from jax.experimental.pallas import tpu as pltpu
from jax.sharding import PartitionSpec as P

SUBS = 6
TILE = 128
LEARN_RATE = 0.05
DECAY = 0.02
NEG_WEIGHT = 0.25
MESH = pl.DeviceIdType.MESH
F32 = jnp.float32
BF16 = jnp.bfloat16


def flipped(index, bit):
    step = 2**bit
    return index + step - 2 * step * ((index // step) % 2)


def as_column(row):
    n = row.shape[1]
    full = jnp.broadcast_to(row, (n, n))
    diagonal = lax.broadcasted_iota(jnp.int32, (n, n), 0) == lax.broadcasted_iota(
        jnp.int32, (n, n), 1
    )
    return jnp.sum(jnp.where(diagonal, full, 0), axis=1, keepdims=True)


def one_hot_rows(column, live, tiles):
    return jnp.concatenate(
        [jnp.where(column == tile, live, 0.0) for tile in range(tiles)], axis=1
    )


def dot(a, b, ca, cb):
    return lax.dot_general(a, b, (((ca,), (cb,)), ((), ())), preferred_element_type=F32)


def kernel(
    n_blk,
    users_in,
    user_accum_in,
    items_in,
    item_accum_in,
    seen_user_in,
    seen_item_in,
    row_live_in,
    col_live_in,
    neg_user_in,
    neg_item_in,
    users_out,
    user_accum_out,
    items_out,
    item_accum_out,
    state,
    lent,
    made,
    given,
    ub,
    vb,
    grad_users,
    grad_items,
    rows,
    cols,
    seen_user_ref,
    seen_item_ref,
    row_live_ref,
    col_live_ref,
    neg_user_ref,
    neg_item_ref,
    send_sem,
    recv_sem,
    load_sem,
):
    blk = lax.axis_index("blk")
    xor = lax.axis_index("xor")
    parity = lax.rem(blk, 2)

    def at(by):
        return lax.rem(blk + n_blk + by, n_blk)

    swap0, swap1 = flipped(xor, 0), flipped(xor, 1)
    swap01 = flipped(swap0, 1)
    barrier = pltpu.get_barrier_semaphore()

    def greet(by, others):
        for other in others:
            pl.semaphore_signal(
                barrier, inc=1, device_id=(at(by), other), device_id_type=MESH
            )

    greet(-2, (xor, swap01))
    greet(-1, (xor, swap0, swap1))

    @pl.when(parity == 0)
    def _():
        greet(1, (xor, swap1))

    n_users, width = users_in.shape
    half = items_in.shape[0] // 2
    block = 256
    n_obs = seen_user_ref.shape[1]
    n_neg = neg_user_ref.shape[1]
    pad = rows.shape[0] - n_obs - n_neg

    halves = [pl.ds(h * half, half) for h in range(2)]
    pairs = (
        (users_in, users_out),
        (items_in.at[halves[0]], state.at[0, 0, 0]),
        (seen_user_in, seen_user_ref),
        (seen_item_in, seen_item_ref),
        (row_live_in, row_live_ref),
        (col_live_in, col_live_ref),
        (neg_user_in, neg_user_ref),
        (neg_item_in, neg_item_ref),
        (item_accum_in.at[halves[0]], state.at[0, 0, 1]),
        (items_in.at[halves[1]], state.at[0, 1, 0]),
        (item_accum_in.at[halves[1]], state.at[0, 1, 1]),
        (user_accum_in, user_accum_out),
    )
    loads = [
        pltpu.make_async_copy(source, target, load_sem.at[i])
        for i, (source, target) in enumerate(pairs)
    ]
    for load in loads:
        load.start()
    for load in loads[2:8]:
        load.wait()

    def masks(s):
        user_tiles, item_tiles = n_users // TILE, 2 * half // TILE
        root = jnp.full((n_neg, TILE), NEG_WEIGHT**0.5, F32)
        for index, negative, live, out, tiles in (
            (seen_user_ref, neg_user_ref, row_live_ref, rows, user_tiles),
            (seen_item_ref, neg_item_ref, col_live_ref, cols, item_tiles),
        ):
            observed = one_hot_rows(
                as_column(index[pl.ds(s, 1), :]), live[s].astype(F32), tiles
            )
            sampled = one_hot_rows(as_column(negative[pl.ds(s, 1), :]), root, tiles)
            out[...] = jnp.concatenate(
                [observed, sampled, jnp.zeros((pad, tiles * TILE), F32)], axis=0
            ).astype(BF16)

    def remote(source, target, kind, c, h, device):
        return pltpu.make_async_remote_copy(
            src_ref=source,
            dst_ref=target,
            send_sem=send_sem.at[c, kind, h],
            recv_sem=recv_sem.at[c, kind, h],
            device_id=device,
            device_id_type=MESH,
        )

    def factor_on(c, h):
        to = (at(2), xor if h == 0 else swap01)
        return remote(state.at[c, h, 0], state.at[c + 1, h, 0], 0, c, h, to)

    def accum_on(c, h):
        to = (at(2), xor if h == 0 else swap01)
        return remote(state.at[c, h, 1], state.at[c + 1, h, 1], 1, c, h, to)

    def lend(c, h):
        to = (at(1), xor if h == 0 else swap0)
        return remote(state.at[c, h, 0], lent.at[c, h], 2, c, h, to)

    def lend_back(c, h):
        to = (at(-1), xor if h == 0 else swap1)
        return remote(state.at[c + 1, h, 0], lent.at[c, h], 2, c, h, to)

    def give_grad(c, h):
        to = (at(1), xor if h == 0 else swap1)
        return remote(made.at[c, h], given.at[c, h], 3, c, h, to)

    def last_move(h):
        to = (at(1), xor if h == 0 else swap0)
        return remote(state.at[2, h], state.at[3, h], 0, 2, h, to)

    def work(h, factor, grad):
        vb[...] = factor[...].astype(BF16)
        grad[...] = DECAY * factor[...]

        def terms(u, carry):
            span = pl.ds(pl.multiple_of(u * block, block), block)
            scores = dot(ub[span], vb[...], 1, 1)
            weight = dot(rows[:, span], cols[:, halves[h]], 0, 0)
            seen = dot(rows[:n_obs, span], cols[:n_obs, halves[h]], 0, 0)
            err = (weight * scores - seen).astype(BF16)
            user_terms = dot(err, vb[...], 1, 0)
            if h == 0:
                grad_users[span] = user_terms
            else:
                grad_users[span] += user_terms
            grad[...] += dot(err, ub[span], 0, 0)
            return carry

        lax.fori_loop(0, n_users // block, terms, 0)

    def adagrad(factor, accum, grad_ref, new_factor, new_accum):
        grad = grad_ref[...]
        summed = accum[...] + grad * grad
        new_accum[...] = summed
        new_factor[...] = factor[...] - LEARN_RATE * grad * lax.rsqrt(summed)

    def update_users():
        def update(u, carry):
            span = pl.ds(pl.multiple_of(u * block, block), block)
            now = users_out[span]
            grad = grad_users[span] + DECAY * now
            summed = user_accum_out[span] + grad * grad
            user_accum_out[span] = summed
            now = now - LEARN_RATE * grad * lax.rsqrt(summed)
            users_out[span] = now
            ub[span] = now.astype(BF16)
            return carry

        lax.fori_loop(0, n_users // block, update, 0)

    cycles = SUBS // 2 - 1
    for c in range(cycles + 1):
        masks(2 * c)
        if c == 0:
            loads[0].wait()
            ub[...] = users_out[...].astype(BF16)
        for h in range(2):
            factor, accum = state.at[c, h, 0], state.at[c, h, 1]
            if c == 0:
                loads[1 if h == 0 else 9].wait()
            else:
                accum_on(c - 1, h).wait_recv()
                lend(c - 1, h).wait_send()
                give_grad(c - 1, h).wait_recv()
                adagrad(factor, accum, given.at[c - 1, h], factor, accum)
            work(h, factor, grad_items)
            if c == 0:
                loads[8 if h == 0 else 10].wait()
            adagrad(factor, accum, grad_items, factor, accum)
            if c == 0 and h == 0:
                pl.semaphore_wait(barrier, 5 + 2 * parity)
            if c == cycles:
                last_move(h).start()
            else:

                @pl.when(parity == 0)
                def _(c=c, h=h):
                    lend(c, h).start()

                factor_on(c, h).start()
        if c < cycles:
            accum_on(c, 0).start()
            accum_on(c, 1).start()
        if c == 0:
            loads[11].wait()
        update_users()
        if c == cycles:
            break

        masks(2 * c + 1)
        for h in range(2):
            factor_on(c, h).wait_recv()

            @pl.when(parity == 1)
            def _(c=c, h=h):
                lend_back(c, h).start()

            lend(c, h).wait_recv()
            work(h, lent.at[c, h], made.at[c, h])
            give_grad(c, h).start()
        update_users()

    masks(SUBS - 1)
    for h in range(2):
        last_move(h).wait_recv()
        factor, accum = state.at[cycles + 1, h, 0], state.at[cycles + 1, h, 1]
        work(h, factor, grad_items)
        here = halves[h]
        adagrad(factor, accum, grad_items, items_out.at[here], item_accum_out.at[here])
    update_users()

    for h in range(2):
        for c in range(cycles):
            factor_on(c, h).wait_send()
            accum_on(c, h).wait_send()
            give_grad(c, h).wait_send()
        last_move(h).wait_send()


def per_device(n_blk, *args):
    users, _, items = args[:3]
    n_users, width = users.shape
    n_items = items.shape[0]
    half = n_items // 2
    entries = -(-(args[4].shape[1] + args[8].shape[1]) // 16) * 16
    vmem = pl.BlockSpec(memory_space=pltpu.VMEM)
    flops = SUBS * 2 * 3 * n_users * n_items * width
    return pl.pallas_call(
        functools.partial(kernel, n_blk),
        out_shape=(
            jax.ShapeDtypeStruct(users.shape, F32),
            jax.ShapeDtypeStruct(users.shape, F32),
            jax.ShapeDtypeStruct(items.shape, F32),
            jax.ShapeDtypeStruct(items.shape, F32),
        ),
        in_specs=[pl.BlockSpec(memory_space=pl.ANY)] * 10,
        out_specs=(vmem,) * 4,
        scratch_shapes=[
            pltpu.VMEM((SUBS // 2 + 1, 2, 2, half, width), F32),
            *[pltpu.VMEM((SUBS // 2 - 1, 2, half, width), F32)] * 3,
            pltpu.VMEM((n_users, width), BF16),
            pltpu.VMEM((half, width), BF16),
            pltpu.VMEM((n_users, width), F32),
            pltpu.VMEM((half, width), F32),
            pltpu.VMEM((entries, n_users), BF16),
            pltpu.VMEM((entries, n_items), BF16),
            *[pltpu.VMEM(arg.shape, arg.dtype) for arg in args[4:]],
            pltpu.SemaphoreType.DMA((SUBS // 2, 4, 2)),
            pltpu.SemaphoreType.DMA((SUBS // 2, 4, 2)),
            pltpu.SemaphoreType.DMA((12,)),
        ],
        compiler_params=pltpu.CompilerParams(
            collective_id=0, has_side_effects=True, vmem_limit_bytes=56 * 2**20
        ),
        cost_estimate=pl.CostEstimate(
            flops=flops, bytes_accessed=12 * 2**20, transcendentals=0
        ),
    )(*args)


def solution(mesh):
    flat = P(("blk", "xor"), None)
    tiles = P(None, ("blk", "xor"))
    live = P(None, ("blk", "xor"), None)
    return jax.shard_map(
        functools.partial(per_device, mesh.shape["blk"]),
        mesh=mesh,
        in_specs=(flat, flat, flat, flat, tiles, tiles, live, live, tiles, tiles),
        out_specs=(flat, flat, flat, flat),
        check_vma=False,
    )
```

time: 137 us -> 128 us (0.934)
  the two profiles are of different devices: /device:TPU:1 before, /device:TPU:6 now
where the time goes in v1:
time: 128 us
  Pallas kernels  121 us (95%)
  local copies, waits for them, and re-layouts  5.77 us (5%)
    pallas_call x1, Pallas kernels, per_device(): pl.pallas_call(functools.partial(kernel, n_blk), out_shape=(jax.ShapeDtyp...  121 us
    unnamed x10, local copies, waits for them, and re-layouts  5.77 us

profile of v1, /device:TPU:6, one launch (start us, length us, event | category | flops | bytes accessed | tf_op | source)
XLA Modules:
  0.0 127.9 jit_solution(14221884597003475037)
XLA Ops:
  0.6 121.5 %shard_map.129 = (f32[1024,256]{1,0:T(8,128)}, f32[1024,256]{1,0:T(8,128)}, f32[512,256]{1,0:T(8,128)}, f32[512,256]{1,0:T(8,128)}) custom-call(f32[1024,256]{1,0:T(8,128)} %users_in.1, f32[1024,256]{1,0:T(8,128)} %user_accum_in.1, f32[512,256]{1,0:T(8,128)} %items_in.1, f32[512,256]{1,0:T(8,128)} %item_accum_in.1, s32[6,16]{1,0:T(8,128)} %seen_user_in.1, ...), custom_call_target="tpu_custom_call" | custom-call | flops 4831838208 | bytes 12582912 | tf_op jit(solution)/shard_map/pallas_call | solution.py:301
  122.1 0.0 copy-start
  122.1 2.4 %copy.18 = f32[1024,256]{1,0:T(8,128)} copy(f32[1024,256]{1,0:T(8,128)} %get-tuple-element.8) | data formatting | bytes 2097152
  124.5 0.0 copy-done
  124.5 0.0 copy-start.2
  124.5 1.0 copy.19
  125.5 0.4 copy-done.2
  125.9 0.0 copy-start.1
  125.9 0.8 copy.20
  126.7 0.4 copy-done.1
  127.1 0.8 copy.21
Async XLA Ops:
  122.1 2.4 %copy-start = (f32[1024,256]{1,0:T(8,128)S(1)}, f32[1024,256]{1,0:T(8,128)}, u32[]{:S(2)}) copy-start(f32[1024,256]{1,0:T(8,128)} %get-tuple-element.9) | copy-start | bytes 3145732
  124.5 1.4 %copy-start.2 = (f32[512,256]{1,0:T(8,128)S(1)}, f32[512,256]{1,0:T(8,128)}, u32[]{:S(2)}) copy-start(f32[512,256]{1,0:T(8,128)} %get-tuple-element.10) | copy-start | bytes 1572868
  125.9 1.2 copy-start.1

commit v2 on v1

--- a/solution.py
+++ b/solution.py
@@ -12,6 +12,7 @@
 LEARN_RATE = 0.05
 DECAY = 0.02
 NEG_WEIGHT = 0.25
+PARTS = 2
 MESH = pl.DeviceIdType.MESH
 F32 = jnp.float32
 BF16 = jnp.bfloat16
@@ -251,9 +252,6 @@
                     lend(c, h).start()
 
                 factor_on(c, h).start()
-        if c < cycles:
-            accum_on(c, 0).start()
-            accum_on(c, 1).start()
         if c == 0:
             loads[11].wait()
         update_users()
@@ -271,6 +269,11 @@
             lend(c, h).wait_recv()
             work(h, lent.at[c, h], made.at[c, h])
             give_grad(c, h).start()
+            if h == 0:
+                for i in range(2):
+                    factor_on(c, i).wait_send()
+                for i in range(2):
+                    accum_on(c, i).start()
         update_users()
 
     masks(SUBS - 1)
@@ -284,10 +287,25 @@
 
     for h in range(2):
         for c in range(cycles):
-            factor_on(c, h).wait_send()
             accum_on(c, h).wait_send()
             give_grad(c, h).wait_send()
         last_move(h).wait_send()
+
+
+def write_out(*refs):
+    sources, targets, sems = refs[:4], refs[4:8], refs[8]
+    copies = []
+    for i, (source, target) in enumerate(zip(sources, targets)):
+        n = source.shape[0] // PARTS
+        for part in range(PARTS):
+            span = pl.ds(part * n, n)
+            copies.append(
+                pltpu.make_async_copy(source.at[span], target.at[span], sems.at[i, part])
+            )
+    for copy in copies:
+        copy.start()
+    for copy in copies:
+        copy.wait()
 
 
 def per_device(n_blk, *args):
@@ -298,7 +316,7 @@
     entries = -(-(args[4].shape[1] + args[8].shape[1]) // 16) * 16
     vmem = pl.BlockSpec(memory_space=pltpu.VMEM)
     flops = SUBS * 2 * 3 * n_users * n_items * width
-    return pl.pallas_call(
+    results = pl.pallas_call(
         functools.partial(kernel, n_blk),
         out_shape=(
             jax.ShapeDtypeStruct(users.shape, F32),
@@ -329,6 +347,18 @@
             flops=flops, bytes_accessed=12 * 2**20, transcendentals=0
         ),
     )(*args)
+    anywhere = pl.BlockSpec(memory_space=pl.ANY)
+    return pl.pallas_call(
+        write_out,
+        out_shape=[jax.ShapeDtypeStruct(x.shape, x.dtype) for x in results],
+        in_specs=[anywhere] * 4,
+        out_specs=[anywhere] * 4,
+        scratch_shapes=[pltpu.SemaphoreType.DMA((4, PARTS))],
+        compiler_params=pltpu.CompilerParams(vmem_limit_bytes=56 * 2**20),
+        cost_estimate=pl.CostEstimate(
+            flops=0, bytes_accessed=6 * 2**20, transcendentals=0
+        ),
+    )(*results)
 
 
 def solution(mesh):

time: 128 us -> 203 us (1.59)
  the two profiles are of different devices: /device:TPU:6 before, /device:TPU:1 now
where the time goes in v2:
time: 203 us; the launch traced here: 202 us
  Pallas kernels  201 us (99%)
    pallas_call x1, Pallas kernels, per_device(): pl.pallas_call(functools.partial(kernel, n_blk), out_shape=(jax.ShapeDtyp...  105 us
    pallas_call x1, Pallas kernels, per_device(): pl.pallas_call(write_out, out_shape=[jax.ShapeDtypeStruct(x.shape, x.dtyp...  96.5 us

profile of v2, /device:TPU:1, one launch (start us, length us, event | category | flops | bytes accessed | tf_op | source)
XLA Modules:
  0.0 201.8 jit_solution(7161214170676729327)
XLA Ops:
  0.6 104.7 %shard_map.129 = (f32[1024,256]{1,0:T(8,128)}, f32[1024,256]{1,0:T(8,128)}, f32[512,256]{1,0:T(8,128)}, f32[512,256]{1,0:T(8,128)}) custom-call(f32[1024,256]{1,0:T(8,128)} %users_in.1, f32[1024,256]{1,0:T(8,128)} %user_accum_in.1, f32[512,256]{1,0:T(8,128)} %items_in.1, f32[512,256]{1,0:T(8,128)} %item_accum_in.1, s32[6,16]{1,0:T(8,128)} %seen_user_in.1, ...), custom_call_target="tpu_custom_call" | custom-call | flops 4831838208 | bytes 12582912 | tf_op jit(solution)/shard_map/pallas_call | solution.py:319
  105.4 96.5 %shard_map.130 = (f32[1024,256]{1,0:T(8,128)}, f32[1024,256]{1,0:T(8,128)}, f32[512,256]{1,0:T(8,128)}, f32[512,256]{1,0:T(8,128)}) custom-call(f32[1024,256]{1,0:T(8,128)} %get-tuple-element.8.refs_0_, f32[1024,256]{1,0:T(8,128)} %get-tuple-element.9.refs_1_, f32[512,256]{1,0:T(8,128)} %get-tuple-element.10.refs_2_, f32[512,256]{1,0:T(8,128)} %get-tuple-element.11.refs_3_), custom_call_target="tpu_custom_call" | custom-call | bytes 6291456 | tf_op jit(solution)/shard_map/pallas_call | solution.py:351

commit v3 on v2

--- a/solution.py
+++ b/solution.py
@@ -58,6 +58,8 @@
     user_accum_out,
     items_out,
     item_accum_out,
+    users,
+    user_accum,
     state,
     lent,
     made,
@@ -68,6 +70,8 @@
     grad_items,
     rows,
     cols,
+    weight,
+    seen,
     seen_user_ref,
     seen_item_ref,
     row_live_ref,
@@ -77,6 +81,7 @@
     send_sem,
     recv_sem,
     load_sem,
+    store_sem,
 ):
     blk = lax.axis_index("blk")
     xor = lax.axis_index("xor")
@@ -111,7 +116,7 @@
 
     halves = [pl.ds(h * half, half) for h in range(2)]
     pairs = (
-        (users_in, users_out),
+        (users_in, users),
         (items_in.at[halves[0]], state.at[0, 0, 0]),
         (seen_user_in, seen_user_ref),
         (seen_item_in, seen_item_ref),
@@ -122,7 +127,7 @@
         (item_accum_in.at[halves[0]], state.at[0, 0, 1]),
         (items_in.at[halves[1]], state.at[0, 1, 0]),
         (item_accum_in.at[halves[1]], state.at[0, 1, 1]),
-        (user_accum_in, user_accum_out),
+        (user_accum_in, user_accum),
     )
     loads = [
         pltpu.make_async_copy(source, target, load_sem.at[i])
@@ -148,39 +153,52 @@
                 [observed, sampled, jnp.zeros((pad, tiles * TILE), F32)], axis=0
             ).astype(BF16)
 
-    def remote(source, target, kind, c, h, device):
+        def spread(u, carry):
+            span = pl.ds(pl.multiple_of(u * block, block), block)
+            weight[span] = dot(rows[:, span], cols[...], 0, 0).astype(BF16)
+            seen[span] = dot(rows[:n_obs, span], cols[:n_obs], 0, 0).astype(BF16)
+            return carry
+
+        lax.fori_loop(0, n_users // block, spread, 0)
+
+    def remote(source, target, kind, c, h, device, part=0):
         return pltpu.make_async_remote_copy(
             src_ref=source,
             dst_ref=target,
-            send_sem=send_sem.at[c, kind, h],
-            recv_sem=recv_sem.at[c, kind, h],
+            send_sem=send_sem.at[c, kind, h, part],
+            recv_sem=recv_sem.at[c, kind, h, part],
             device_id=device,
             device_id_type=MESH,
         )
 
-    def factor_on(c, h):
+    spans = [pl.ds(i * (half // PARTS), half // PARTS) for i in range(PARTS)]
+
+    def factor_on(c, h, i):
         to = (at(2), xor if h == 0 else swap01)
-        return remote(state.at[c, h, 0], state.at[c + 1, h, 0], 0, c, h, to)
+        source, target = state.at[c, h, 0, spans[i]], state.at[c + 1, h, 0, spans[i]]
+        return remote(source, target, 0, c, h, to, i)
 
     def accum_on(c, h):
         to = (at(2), xor if h == 0 else swap01)
         return remote(state.at[c, h, 1], state.at[c + 1, h, 1], 1, c, h, to)
 
-    def lend(c, h):
+    def lend(c, h, i):
         to = (at(1), xor if h == 0 else swap0)
-        return remote(state.at[c, h, 0], lent.at[c, h], 2, c, h, to)
-
-    def lend_back(c, h):
+        source, target = state.at[c, h, 0, spans[i]], lent.at[c, h, spans[i]]
+        return remote(source, target, 2, c, h, to, i)
+
+    def lend_back(c, h, i):
         to = (at(-1), xor if h == 0 else swap1)
-        return remote(state.at[c + 1, h, 0], lent.at[c, h], 2, c, h, to)
+        source, target = state.at[c + 1, h, 0, spans[i]], lent.at[c, h, spans[i]]
+        return remote(source, target, 2, c, h, to, i)
 
     def give_grad(c, h):
         to = (at(1), xor if h == 0 else swap1)
         return remote(made.at[c, h], given.at[c, h], 3, c, h, to)
 
-    def last_move(h):
+    def last_move(h, kind):
         to = (at(1), xor if h == 0 else swap0)
-        return remote(state.at[2, h], state.at[3, h], 0, 2, h, to)
+        return remote(state.at[2, h, kind], state.at[3, h, kind], kind, 2, h, to)
 
     def work(h, factor, grad):
         vb[...] = factor[...].astype(BF16)
@@ -189,9 +207,8 @@
         def terms(u, carry):
             span = pl.ds(pl.multiple_of(u * block, block), block)
             scores = dot(ub[span], vb[...], 1, 1)
-            weight = dot(rows[:, span], cols[:, halves[h]], 0, 0)
-            seen = dot(rows[:n_obs, span], cols[:n_obs, halves[h]], 0, 0)
-            err = (weight * scores - seen).astype(BF16)
+            weighted = weight[span, halves[h]].astype(F32) * scores
+            err = (weighted - seen[span, halves[h]].astype(F32)).astype(BF16)
             user_terms = dot(err, vb[...], 1, 0)
             if h == 0:
                 grad_users[span] = user_terms
@@ -200,58 +217,61 @@
             grad[...] += dot(err, ub[span], 0, 0)
             return carry
 
-        lax.fori_loop(0, n_users // block, terms, 0)
-
-    def adagrad(factor, accum, grad_ref, new_factor, new_accum):
+        lax.fori_loop(0, n_users // block, terms, 0, unroll=True)
+
+    def adagrad(factor, accum, grad_ref):
         grad = grad_ref[...]
         summed = accum[...] + grad * grad
-        new_accum[...] = summed
-        new_factor[...] = factor[...] - LEARN_RATE * grad * lax.rsqrt(summed)
+        accum[...] = summed
+        factor[...] = factor[...] - LEARN_RATE * grad * lax.rsqrt(summed)
 
     def update_users():
         def update(u, carry):
             span = pl.ds(pl.multiple_of(u * block, block), block)
-            now = users_out[span]
+            now = users[span]
             grad = grad_users[span] + DECAY * now
-            summed = user_accum_out[span] + grad * grad
-            user_accum_out[span] = summed
+            summed = user_accum[span] + grad * grad
+            user_accum[span] = summed
             now = now - LEARN_RATE * grad * lax.rsqrt(summed)
-            users_out[span] = now
+            users[span] = now
             ub[span] = now.astype(BF16)
             return carry
 
-        lax.fori_loop(0, n_users // block, update, 0)
+        lax.fori_loop(0, n_users // block, update, 0, unroll=True)
 
     cycles = SUBS // 2 - 1
     for c in range(cycles + 1):
         masks(2 * c)
         if c == 0:
             loads[0].wait()
-            ub[...] = users_out[...].astype(BF16)
+            ub[...] = users[...].astype(BF16)
         for h in range(2):
             factor, accum = state.at[c, h, 0], state.at[c, h, 1]
             if c == 0:
                 loads[1 if h == 0 else 9].wait()
             else:
                 accum_on(c - 1, h).wait_recv()
-                lend(c - 1, h).wait_send()
+                for i in range(PARTS):
+                    lend(c - 1, h, i).wait_send()
                 give_grad(c - 1, h).wait_recv()
-                adagrad(factor, accum, given.at[c - 1, h], factor, accum)
-            work(h, factor, grad_items)
+                adagrad(factor, accum, given.at[c - 1, h])
+            work(h, factor, grad_items.at[h])
             if c == 0:
                 loads[8 if h == 0 else 10].wait()
-            adagrad(factor, accum, grad_items, factor, accum)
+            adagrad(factor, accum, grad_items.at[h])
             if c == 0 and h == 0:
                 pl.semaphore_wait(barrier, 5 + 2 * parity)
             if c == cycles:
-                last_move(h).start()
+                last_move(h, 0).start()
             else:
 
                 @pl.when(parity == 0)
                 def _(c=c, h=h):
-                    lend(c, h).start()
-
-                factor_on(c, h).start()
+                    for i in range(PARTS):
+                        lend(c, h, i).start()
+
+                for i in range(PARTS):
+                    factor_on(c, h, i).start()
         if c == 0:
             loads[11].wait()
         update_users()
@@ -260,52 +280,86 @@
 
         masks(2 * c + 1)
         for h in range(2):
-            factor_on(c, h).wait_recv()
-
-            @pl.when(parity == 1)
-            def _(c=c, h=h):
-                lend_back(c, h).start()
-
-            lend(c, h).wait_recv()
+            for i in range(PARTS):
+                factor_on(c, h, i).wait_recv()
+
+                @pl.when(parity == 1)
+                def _(c=c, h=h, i=i):
+                    lend_back(c, h, i).start()
+
+            if h == 1:
+                for k in range(2):
+                    for i in range(PARTS):
+                        factor_on(c, k, i).wait_send()
+                for k in range(2):
+                    accum_on(c, k).start()
+            for i in range(PARTS):
+                lend(c, h, i).wait_recv()
             work(h, lent.at[c, h], made.at[c, h])
             give_grad(c, h).start()
-            if h == 0:
-                for i in range(2):
-                    factor_on(c, i).wait_send()
-                for i in range(2):
-                    accum_on(c, i).start()
         update_users()
 
     masks(SUBS - 1)
     for h in range(2):
-        last_move(h).wait_recv()
+        last_move(h, 0).wait_send()
+        last_move(h, 1).start()
+        last_move(h, 0).wait_recv()
+        work(h, state.at[cycles + 1, h, 0], grad_items.at[h])
+    update_users()
+    stores = [
+        pltpu.make_async_copy(users, users_out, store_sem.at[0]),
+        pltpu.make_async_copy(user_accum, user_accum_out, store_sem.at[1]),
+    ]
+    for store in stores:
+        store.start()
+    for h in range(2):
+        last_move(h, 1).wait_recv()
         factor, accum = state.at[cycles + 1, h, 0], state.at[cycles + 1, h, 1]
-        work(h, factor, grad_items)
-        here = halves[h]
-        adagrad(factor, accum, grad_items, items_out.at[here], item_accum_out.at[here])
-    update_users()
+        adagrad(factor, accum, grad_items.at[h])
+        for i, (source, target) in enumerate(
+            ((factor, items_out), (accum, item_accum_out))
+        ):
+            store = pltpu.make_async_copy(
+                source, target.at[halves[h]], store_sem.at[2 + 2 * h + i]
+            )
+            store.start()
+            stores.append(store)
 
     for h in range(2):
         for c in range(cycles):
             accum_on(c, h).wait_send()
             give_grad(c, h).wait_send()
-        last_move(h).wait_send()
+        last_move(h, 1).wait_send()
+    for store in stores:
+        store.wait()
 
 
 def write_out(*refs):
-    sources, targets, sems = refs[:4], refs[4:8], refs[8]
-    copies = []
-    for i, (source, target) in enumerate(zip(sources, targets)):
+    sources, targets, buffers, (load_sem, store_sem) = (
+        refs[:4],
+        refs[4:8],
+        refs[8:12],
+        refs[12:],
+    )
+    loads, stores = [], []
+    for i, (source, target, buffer) in enumerate(zip(sources, targets, buffers)):
         n = source.shape[0] // PARTS
         for part in range(PARTS):
             span = pl.ds(part * n, n)
-            copies.append(
-                pltpu.make_async_copy(source.at[span], target.at[span], sems.at[i, part])
+            sems = load_sem.at[i, part], store_sem.at[i, part]
+            loads.append(
+                pltpu.make_async_copy(source.at[span], buffer.at[span], sems[0])
             )
-    for copy in copies:
-        copy.start()
-    for copy in copies:
-        copy.wait()
+            stores.append(
+                pltpu.make_async_copy(buffer.at[span], target.at[span], sems[1])
+            )
+    for load in loads:
+        load.start()
+    for load, store in zip(loads, stores):
+        load.wait()
+        store.start()
+    for store in stores:
+        store.wait()
 
 
 def per_device(n_blk, *args):
@@ -314,7 +368,7 @@
     n_items = items.shape[0]
     half = n_items // 2
     entries = -(-(args[4].shape[1] + args[8].shape[1]) // 16) * 16
-    vmem = pl.BlockSpec(memory_space=pltpu.VMEM)
+    anywhere = pl.BlockSpec(memory_space=pl.ANY)
     flops = SUBS * 2 * 3 * n_users * n_items * width
     results = pl.pallas_call(
         functools.partial(kernel, n_blk),
@@ -324,21 +378,26 @@
             jax.ShapeDtypeStruct(items.shape, F32),
             jax.ShapeDtypeStruct(items.shape, F32),
         ),
-        in_specs=[pl.BlockSpec(memory_space=pl.ANY)] * 10,
-        out_specs=(vmem,) * 4,
+        in_specs=[anywhere] * 10,
+        out_specs=(anywhere,) * 4,
         scratch_shapes=[
+            pltpu.VMEM((n_users, width), F32),
+            pltpu.VMEM((n_users, width), F32),
             pltpu.VMEM((SUBS // 2 + 1, 2, 2, half, width), F32),
             *[pltpu.VMEM((SUBS // 2 - 1, 2, half, width), F32)] * 3,
             pltpu.VMEM((n_users, width), BF16),
             pltpu.VMEM((half, width), BF16),
             pltpu.VMEM((n_users, width), F32),
-            pltpu.VMEM((half, width), F32),
+            pltpu.VMEM((2, half, width), F32),
             pltpu.VMEM((entries, n_users), BF16),
             pltpu.VMEM((entries, n_items), BF16),
+            pltpu.VMEM((n_users, n_items), BF16),
+            pltpu.VMEM((n_users, n_items), BF16),
             *[pltpu.VMEM(arg.shape, arg.dtype) for arg in args[4:]],
-            pltpu.SemaphoreType.DMA((SUBS // 2, 4, 2)),
-            pltpu.SemaphoreType.DMA((SUBS // 2, 4, 2)),
+            pltpu.SemaphoreType.DMA((SUBS // 2, 4, 2, PARTS)),
+            pltpu.SemaphoreType.DMA((SUBS // 2, 4, 2, PARTS)),
             pltpu.SemaphoreType.DMA((12,)),
+            pltpu.SemaphoreType.DMA((6,)),
         ],
         compiler_params=pltpu.CompilerParams(
             collective_id=0, has_side_effects=True, vmem_limit_bytes=56 * 2**20
@@ -347,13 +406,16 @@
             flops=flops, bytes_accessed=12 * 2**20, transcendentals=0
         ),
     )(*args)
-    anywhere = pl.BlockSpec(memory_space=pl.ANY)
     return pl.pallas_call(
         write_out,
         out_shape=[jax.ShapeDtypeStruct(x.shape, x.dtype) for x in results],
         in_specs=[anywhere] * 4,
         out_specs=[anywhere] * 4,
-        scratch_shapes=[pltpu.SemaphoreType.DMA((4, PARTS))],
+        scratch_shapes=[
+            *[pltpu.VMEM(x.shape, x.dtype) for x in results],
+            pltpu.SemaphoreType.DMA((4, PARTS)),
+            pltpu.SemaphoreType.DMA((4, PARTS)),
+        ],
         compiler_params=pltpu.CompilerParams(vmem_limit_bytes=56 * 2**20),
         cost_estimate=pl.CostEstimate(
             flops=0, bytes_accessed=6 * 2**20, transcendentals=0

time: 203 us -> 107 us (0.53)
  Pallas kernels: 201 us -> 105 us
    pallas_call x1, Pallas kernels: 96.5 us -> 2.83 us  [per_device(): pl.pallas_call(write_out, out_shape=[jax.ShapeDtypeStruct(x.shape, x.dtyp...]
    pallas_call x1, Pallas kernels: 105 us -> 102 us  [per_device(): pl.pallas_call(functools.partial(kernel, n_blk), out_shape=(jax.ShapeDtyp...]
where the time goes in v3:
time: 107 us; the launch traced here: 106 us
  Pallas kernels  105 us (98%)
    pallas_call x1, Pallas kernels, per_device(): pl.pallas_call(functools.partial(kernel, n_blk), out_shape=(jax.ShapeDtyp...  102 us
    pallas_call x1, Pallas kernels, per_device(): pl.pallas_call(write_out, out_shape=[jax.ShapeDtypeStruct(x.shape, x.dtyp...  2.83 us

profile of v3, /device:TPU:1, one launch (start us, length us, event | category | flops | bytes accessed | tf_op | source)
XLA Modules:
  0.0 105.6 jit_solution(9943576881902575056)
XLA Ops:
  0.6 102.1 %shard_map.129 = (f32[1024,256]{1,0:T(8,128)}, f32[1024,256]{1,0:T(8,128)}, f32[512,256]{1,0:T(8,128)}, f32[512,256]{1,0:T(8,128)}) custom-call(f32[1024,256]{1,0:T(8,128)} %users_in.1, f32[1024,256]{1,0:T(8,128)} %user_accum_in.1, f32[512,256]{1,0:T(8,128)} %items_in.1, f32[512,256]{1,0:T(8,128)} %item_accum_in.1, s32[6,16]{1,0:T(8,128)} %seen_user_in.1, ...), custom_call_target="tpu_custom_call" | custom-call | flops 4831838208 | bytes 12582912 | tf_op jit(solution)/shard_map/pallas_call | solution.py:373
  102.8 2.8 %shard_map.130 = (f32[1024,256]{1,0:T(8,128)}, f32[1024,256]{1,0:T(8,128)}, f32[512,256]{1,0:T(8,128)}, f32[512,256]{1,0:T(8,128)}) custom-call(f32[1024,256]{1,0:T(8,128)} %get-tuple-element.8.refs_0_, f32[1024,256]{1,0:T(8,128)} %get-tuple-element.9.refs_1_, f32[512,256]{1,0:T(8,128)} %get-tuple-element.10.refs_2_, f32[512,256]{1,0:T(8,128)} %get-tuple-element.11.refs_3_), custom_call_target="tpu_custom_call" | custom-call | bytes 6291456 | tf_op jit(solution)/shard_map/pallas_call | solution.py:409

commit v4 on v3

--- a/solution.py
+++ b/solution.py
@@ -61,9 +61,7 @@
     users,
     user_accum,
     state,
-    lent,
-    made,
-    given,
+    relay,
     ub,
     vb,
     grad_users,
@@ -80,6 +78,8 @@
     neg_item_ref,
     send_sem,
     recv_sem,
+    relay_send,
+    relay_recv,
     load_sem,
     store_sem,
 ):
@@ -91,7 +91,6 @@
         return lax.rem(blk + n_blk + by, n_blk)
 
     swap0, swap1 = flipped(xor, 0), flipped(xor, 1)
-    swap01 = flipped(swap0, 1)
     barrier = pltpu.get_barrier_semaphore()
 
     def greet(by, others):
@@ -100,12 +99,15 @@
                 barrier, inc=1, device_id=(at(by), other), device_id_type=MESH
             )
 
-    greet(-2, (xor, swap01))
-    greet(-1, (xor, swap0, swap1))
-
     @pl.when(parity == 0)
     def _():
-        greet(1, (xor, swap1))
+        greet(1, (xor, swap0, swap1))
+        greet(-2, (xor, swap0, swap1))
+
+    @pl.when(parity == 1)
+    def _():
+        greet(-1, (xor, swap0, swap1))
+        greet(-2, (xor,))
 
     n_users, width = users_in.shape
     half = items_in.shape[0] // 2
@@ -115,20 +117,22 @@
     pad = rows.shape[0] - n_obs - n_neg
 
     halves = [pl.ds(h * half, half) for h in range(2)]
-    pairs = (
+    size = half // PARTS
+    pairs = [
         (users_in, users),
-        (items_in.at[halves[0]], state.at[0, 0, 0]),
+        (user_accum_in, user_accum),
         (seen_user_in, seen_user_ref),
         (seen_item_in, seen_item_ref),
         (row_live_in, row_live_ref),
         (col_live_in, col_live_ref),
         (neg_user_in, neg_user_ref),
         (neg_item_in, neg_item_ref),
-        (item_accum_in.at[halves[0]], state.at[0, 0, 1]),
-        (items_in.at[halves[1]], state.at[0, 1, 0]),
-        (item_accum_in.at[halves[1]], state.at[0, 1, 1]),
-        (user_accum_in, user_accum),
-    )
+    ]
+    for h in range(2):
+        for i in range(PARTS):
+            from_rows = pl.ds(h * half + i * size, size)
+            pairs.append((items_in.at[from_rows], state.at[0, h, i, 0]))
+            pairs.append((item_accum_in.at[from_rows], state.at[0, h, i, 1]))
     loads = [
         pltpu.make_async_copy(source, target, load_sem.at[i])
         for i, (source, target) in enumerate(pairs)
@@ -161,48 +165,48 @@
 
         lax.fori_loop(0, n_users // block, spread, 0)
 
-    def remote(source, target, kind, c, h, device, part=0):
+    def remote(source, target, sems, device):
         return pltpu.make_async_remote_copy(
             src_ref=source,
             dst_ref=target,
-            send_sem=send_sem.at[c, kind, h, part],
-            recv_sem=recv_sem.at[c, kind, h, part],
+            send_sem=sems[0],
+            recv_sem=sems[1],
             device_id=device,
             device_id_type=MESH,
         )
 
-    spans = [pl.ds(i * (half // PARTS), half // PARTS) for i in range(PARTS)]
-
-    def factor_on(c, h, i):
-        to = (at(2), xor if h == 0 else swap01)
-        source, target = state.at[c, h, 0, spans[i]], state.at[c + 1, h, 0, spans[i]]
-        return remote(source, target, 0, c, h, to, i)
-
-    def accum_on(c, h):
-        to = (at(2), xor if h == 0 else swap01)
-        return remote(state.at[c, h, 1], state.at[c + 1, h, 1], 1, c, h, to)
-
-    def lend(c, h, i):
-        to = (at(1), xor if h == 0 else swap0)
-        source, target = state.at[c, h, 0, spans[i]], lent.at[c, h, spans[i]]
-        return remote(source, target, 2, c, h, to, i)
-
-    def lend_back(c, h, i):
-        to = (at(-1), xor if h == 0 else swap1)
-        source, target = state.at[c + 1, h, 0, spans[i]], lent.at[c, h, spans[i]]
-        return remote(source, target, 2, c, h, to, i)
-
-    def give_grad(c, h):
-        to = (at(1), xor if h == 0 else swap1)
-        return remote(made.at[c, h], given.at[c, h], 3, c, h, to)
-
-    def last_move(h, kind):
-        to = (at(1), xor if h == 0 else swap0)
-        return remote(state.at[2, h, kind], state.at[3, h, kind], kind, 2, h, to)
-
-    def work(h, factor, grad):
-        vb[...] = factor[...].astype(BF16)
-        grad[...] = DECAY * factor[...]
+    def after(s, h):
+        return xor if h == 0 else (swap0 if s % 2 == 0 else swap1)
+
+    def direct(s, h, i):
+        return remote(
+            state.at[s, h, i],
+            state.at[s + 1, h, i],
+            (send_sem.at[s, h, i], recv_sem.at[s, h, i]),
+            (at(1), after(s, h)),
+        )
+
+    def first_hop(s, h, i):
+        return remote(
+            state.at[s, h, i],
+            relay.at[s, h],
+            (send_sem.at[s, h, i], relay_recv.at[s, h]),
+            (at(2) if i == 0 else at(-1), xor),
+        )
+
+    def second_hop(s, h, i):
+        return remote(
+            relay.at[s, h],
+            state.at[s + 1, h, i],
+            (relay_send.at[s, h], recv_sem.at[s, h, i]),
+            (at(-1) if i == 0 else at(2), after(s, h)),
+        )
+
+    def work(h, slot):
+        for i in range(PARTS):
+            factor = state[slot, h, i, 0]
+            vb[pl.ds(i * size, size)] = factor.astype(BF16)
+            grad_items[pl.ds(i * size, size)] = DECAY * factor
 
         def terms(u, carry):
             span = pl.ds(pl.multiple_of(u * block, block), block)
@@ -214,16 +218,16 @@
                 grad_users[span] = user_terms
             else:
                 grad_users[span] += user_terms
-            grad[...] += dot(err, ub[span], 0, 0)
+            grad_items[...] += dot(err, ub[span], 0, 0)
             return carry
 
         lax.fori_loop(0, n_users // block, terms, 0, unroll=True)
 
-    def adagrad(factor, accum, grad_ref):
-        grad = grad_ref[...]
-        summed = accum[...] + grad * grad
-        accum[...] = summed
-        factor[...] = factor[...] - LEARN_RATE * grad * lax.rsqrt(summed)
+    def adagrad(slot, h, i):
+        grad = grad_items[pl.ds(i * size, size)]
+        summed = state[slot, h, i, 1] + grad * grad
+        state[slot, h, i, 1] = summed
+        state[slot, h, i, 0] = state[slot, h, i, 0] - LEARN_RATE * grad * lax.rsqrt(summed)
 
     def update_users():
         def update(u, carry):
@@ -239,97 +243,75 @@
 
         lax.fori_loop(0, n_users // block, update, 0, unroll=True)
 
-    cycles = SUBS // 2 - 1
-    for c in range(cycles + 1):
-        masks(2 * c)
-        if c == 0:
+    def pass_on(s, h, i):
+        first_hop(s, h, i).wait_recv()
+        second_hop(s, h, i).start()
+
+    stores = []
+    for s in range(SUBS):
+        masks(s)
+        if s == 0:
             loads[0].wait()
             ub[...] = users[...].astype(BF16)
+        else:
+
+            @pl.when(parity == 0)
+            def _(s=s):
+                for h in range(2):
+                    pass_on(s - 1, h, 1)
+
         for h in range(2):
-            factor, accum = state.at[c, h, 0], state.at[c, h, 1]
-            if c == 0:
-                loads[1 if h == 0 else 9].wait()
+            if s > 0:
+
+                @pl.when(parity == 1)
+                def _(s=s, h=h):
+                    pass_on(s - 1, h, 0)
+
+                for i in range(PARTS):
+                    direct(s - 1, h, i).wait_recv()
             else:
-                accum_on(c - 1, h).wait_recv()
-                for i in range(PARTS):
-                    lend(c - 1, h, i).wait_send()
-                give_grad(c - 1, h).wait_recv()
-                adagrad(factor, accum, given.at[c - 1, h])
-            work(h, factor, grad_items.at[h])
-            if c == 0:
-                loads[8 if h == 0 else 10].wait()
-            adagrad(factor, accum, grad_items.at[h])
-            if c == 0 and h == 0:
-                pl.semaphore_wait(barrier, 5 + 2 * parity)
-            if c == cycles:
-                last_move(h, 0).start()
-            else:
-
-                @pl.when(parity == 0)
-                def _(c=c, h=h):
-                    for i in range(PARTS):
-                        lend(c, h, i).start()
-
-                for i in range(PARTS):
-                    factor_on(c, h, i).start()
-        if c == 0:
-            loads[11].wait()
+                for load in loads[8 + 4 * h : 12 + 4 * h]:
+                    load.wait()
+            work(h, s)
+            for i in range(PARTS):
+                adagrad(s, h, i)
+                if s == 0 and h == 0 and i == 0:
+                    pl.semaphore_wait(barrier, 6 - 2 * parity)
+                if s < SUBS - 1:
+
+                    @pl.when(parity == 0)
+                    def _(s=s, h=h, i=i):
+                        direct(s, h, i).start()
+
+                    @pl.when(parity == 1)
+                    def _(s=s, h=h, i=i):
+                        first_hop(s, h, i).start()
+
+                else:
+                    to_rows = pl.ds(h * half + i * size, size)
+                    for k, target in enumerate((items_out, item_accum_out)):
+                        store = pltpu.make_async_copy(
+                            state.at[s, h, i, k],
+                            target.at[to_rows],
+                            store_sem.at[2 + 4 * h + 2 * i + k],
+                        )
+                        store.start()
+                        stores.append(store)
+        if s == 0:
+            loads[1].wait()
         update_users()
-        if c == cycles:
-            break
-
-        masks(2 * c + 1)
+    for i, (source, target) in enumerate(
+        ((users, users_out), (user_accum, user_accum_out))
+    ):
+        store = pltpu.make_async_copy(source, target, store_sem.at[i])
+        store.start()
+        stores.append(store)
+
+    for s in range(SUBS - 1):
         for h in range(2):
             for i in range(PARTS):
-                factor_on(c, h, i).wait_recv()
-
-                @pl.when(parity == 1)
-                def _(c=c, h=h, i=i):
-                    lend_back(c, h, i).start()
-
-            if h == 1:
-                for k in range(2):
-                    for i in range(PARTS):
-                        factor_on(c, k, i).wait_send()
-                for k in range(2):
-                    accum_on(c, k).start()
-            for i in range(PARTS):
-                lend(c, h, i).wait_recv()
-            work(h, lent.at[c, h], made.at[c, h])
-            give_grad(c, h).start()
-        update_users()
-
-    masks(SUBS - 1)
-    for h in range(2):
-        last_move(h, 0).wait_send()
-        last_move(h, 1).start()
-        last_move(h, 0).wait_recv()
-        work(h, state.at[cycles + 1, h, 0], grad_items.at[h])
-    update_users()
-    stores = [
-        pltpu.make_async_copy(users, users_out, store_sem.at[0]),
-        pltpu.make_async_copy(user_accum, user_accum_out, store_sem.at[1]),
-    ]
-    for store in stores:
-        store.start()
-    for h in range(2):
-        last_move(h, 1).wait_recv()
-        factor, accum = state.at[cycles + 1, h, 0], state.at[cycles + 1, h, 1]
-        adagrad(factor, accum, grad_items.at[h])
-        for i, (source, target) in enumerate(
-            ((factor, items_out), (accum, item_accum_out))
-        ):
-            store = pltpu.make_async_copy(
-                source, target.at[halves[h]], store_sem.at[2 + 2 * h + i]
-            )
-            store.start()
-            stores.append(store)
-
-    for h in range(2):
-        for c in range(cycles):
-            accum_on(c, h).wait_send()
-            give_grad(c, h).wait_send()
-        last_move(h, 1).wait_send()
+                direct(s, h, i).wait_send()
+            second_hop(s, h, 0).wait_send()
     for store in stores:
         store.wait()
 
@@ -383,21 +365,23 @@
         scratch_shapes=[
             pltpu.VMEM((n_users, width), F32),
             pltpu.VMEM((n_users, width), F32),
-            pltpu.VMEM((SUBS // 2 + 1, 2, 2, half, width), F32),
-            *[pltpu.VMEM((SUBS // 2 - 1, 2, half, width), F32)] * 3,
+            pltpu.VMEM((SUBS, 2, PARTS, 2, half // PARTS, width), F32),
+            pltpu.VMEM((SUBS - 1, 2, 2, half // PARTS, width), F32),
             pltpu.VMEM((n_users, width), BF16),
             pltpu.VMEM((half, width), BF16),
             pltpu.VMEM((n_users, width), F32),
-            pltpu.VMEM((2, half, width), F32),
+            pltpu.VMEM((half, width), F32),
             pltpu.VMEM((entries, n_users), BF16),
             pltpu.VMEM((entries, n_items), BF16),
             pltpu.VMEM((n_users, n_items), BF16),
             pltpu.VMEM((n_users, n_items), BF16),
             *[pltpu.VMEM(arg.shape, arg.dtype) for arg in args[4:]],
-            pltpu.SemaphoreType.DMA((SUBS // 2, 4, 2, PARTS)),
-            pltpu.SemaphoreType.DMA((SUBS // 2, 4, 2, PARTS)),
-            pltpu.SemaphoreType.DMA((12,)),
-            pltpu.SemaphoreType.DMA((6,)),
+            pltpu.SemaphoreType.DMA((SUBS - 1, 2, PARTS)),
+            pltpu.SemaphoreType.DMA((SUBS - 1, 2, PARTS)),
+            pltpu.SemaphoreType.DMA((SUBS - 1, 2)),
+            pltpu.SemaphoreType.DMA((SUBS - 1, 2)),
+            pltpu.SemaphoreType.DMA((8 + 4 * PARTS,)),
+            pltpu.SemaphoreType.DMA((2 + 4 * PARTS,)),
         ],
         compiler_params=pltpu.CompilerParams(
             collective_id=0, has_side_effects=True, vmem_limit_bytes=56 * 2**20

time: 107 us -> 128 us (1.20); the launches traced: 106 us -> 128 us
  Pallas kernels: 105 us -> 127 us
    pallas_call x1, Pallas kernels: 102 us -> 124 us  [per_device(): pl.pallas_call(functools.partial(kernel, n_blk), out_shape=(jax.ShapeDtyp...]
where the time goes in v4:
time: 128 us
  Pallas kernels  127 us (99%)
    pallas_call x1, Pallas kernels, per_device(): pl.pallas_call(functools.partial(kernel, n_blk), out_shape=(jax.ShapeDtyp...  124 us
    pallas_call x1, Pallas kernels, per_device(): pl.pallas_call(write_out, out_shape=[jax.ShapeDtypeStruct(x.shape, x.dtyp...  2.83 us

profile of v4, /device:TPU:1, one launch (start us, length us, event | category | flops | bytes accessed | tf_op | source)
XLA Modules:
  0.0 128.0 jit_solution(5002151824241720029)
XLA Ops:
  0.6 124.5 %shard_map.129 = (f32[1024,256]{1,0:T(8,128)}, f32[1024,256]{1,0:T(8,128)}, f32[512,256]{1,0:T(8,128)}, f32[512,256]{1,0:T(8,128)}) custom-call(f32[1024,256]{1,0:T(8,128)} %users_in.1, f32[1024,256]{1,0:T(8,128)} %user_accum_in.1, f32[512,256]{1,0:T(8,128)} %items_in.1, f32[512,256]{1,0:T(8,128)} %item_accum_in.1, s32[6,16]{1,0:T(8,128)} %seen_user_in.1, ...), custom_call_target="tpu_custom_call" | custom-call | flops 4831838208 | bytes 12582912 | tf_op jit(solution)/shard_map/pallas_call | solution.py:355
  125.1 2.8 %shard_map.130 = (f32[1024,256]{1,0:T(8,128)}, f32[1024,256]{1,0:T(8,128)}, f32[512,256]{1,0:T(8,128)}, f32[512,256]{1,0:T(8,128)}) custom-call(f32[1024,256]{1,0:T(8,128)} %get-tuple-element.8.refs_0_, f32[1024,256]{1,0:T(8,128)} %get-tuple-element.9.refs_1_, f32[512,256]{1,0:T(8,128)} %get-tuple-element.10.refs_2_, f32[512,256]{1,0:T(8,128)} %get-tuple-element.11.refs_3_), custom_call_target="tpu_custom_call" | custom-call | bytes 6291456 | tf_op jit(solution)/shard_map/pallas_call | solution.py:393

commit v5 on v3

--- a/solution.py
+++ b/solution.py
@@ -64,6 +64,7 @@
     lent,
     made,
     given,
+    relay,
     ub,
     vb,
     grad_users,
@@ -80,6 +81,8 @@
     neg_item_ref,
     send_sem,
     recv_sem,
+    relay_send,
+    relay_recv,
     load_sem,
     store_sem,
 ):
@@ -100,7 +103,7 @@
                 barrier, inc=1, device_id=(at(by), other), device_id_type=MESH
             )
 
-    greet(-2, (xor, swap01))
+    greet(-2, (xor, swap1, swap01))
     greet(-1, (xor, swap0, swap1))
 
     @pl.when(parity == 0)
@@ -196,6 +199,39 @@
         to = (at(1), xor if h == 0 else swap1)
         return remote(made.at[c, h], given.at[c, h], 3, c, h, to)
 
+    def grad_hop(c, h):
+        to = (at(2) if h == 0 else at(-1), xor)
+        return pltpu.make_async_remote_copy(
+            src_ref=made.at[c, h],
+            dst_ref=relay.at[c],
+            send_sem=send_sem.at[c, 3, h, 0],
+            recv_sem=relay_recv.at[c],
+            device_id=to,
+            device_id_type=MESH,
+        )
+
+    def remote_pass(c):
+        return pltpu.make_async_remote_copy(
+            src_ref=relay.at[c],
+            dst_ref=given.at[c, 0],
+            send_sem=relay_send.at[c],
+            recv_sem=recv_sem.at[c, 3, 0, 0],
+            device_id=(at(-1), xor),
+            device_id_type=MESH,
+        )
+
+    def pass_grad(c, h):
+        grad_hop(c, h).wait_recv()
+        to = (at(-1), xor) if h == 0 else (at(2), swap1)
+        pltpu.make_async_remote_copy(
+            src_ref=relay.at[c],
+            dst_ref=given.at[c, h],
+            send_sem=relay_send.at[c],
+            recv_sem=recv_sem.at[c, 3, h, 0],
+            device_id=to,
+            device_id_type=MESH,
+        ).start()
+
     def last_move(h, kind):
         to = (at(1), xor if h == 0 else swap0)
         return remote(state.at[2, h, kind], state.at[3, h, kind], kind, 2, h, to)
@@ -260,7 +296,7 @@
                 loads[8 if h == 0 else 10].wait()
             adagrad(factor, accum, grad_items.at[h])
             if c == 0 and h == 0:
-                pl.semaphore_wait(barrier, 5 + 2 * parity)
+                pl.semaphore_wait(barrier, 6 + 2 * parity)
             if c == cycles:
                 last_move(h, 0).start()
             else:
@@ -296,8 +332,25 @@
             for i in range(PARTS):
                 lend(c, h, i).wait_recv()
             work(h, lent.at[c, h], made.at[c, h])
-            give_grad(c, h).start()
+
+            @pl.when(parity == 0)
+            def _(c=c, h=h):
+                give_grad(c, h).start()
+
+            @pl.when(parity == 1)
+            def _(c=c, h=h):
+                grad_hop(c, h).start()
+
         update_users()
+
+        @pl.when(parity == 0)
+        def _(c=c):
+            pass_grad(c, 1)
+
+        @pl.when(parity == 1)
+        def _(c=c):
+            pass_grad(c, 0)
+
 
     masks(SUBS - 1)
     for h in range(2):
@@ -328,6 +381,8 @@
     for h in range(2):
         for c in range(cycles):
             accum_on(c, h).wait_send()
+            if h == 0:
+                remote_pass(c).wait_send()
             give_grad(c, h).wait_send()
         last_move(h, 1).wait_send()
     for store in stores:
@@ -385,6 +440,7 @@
             pltpu.VMEM((n_users, width), F32),
             pltpu.VMEM((SUBS // 2 + 1, 2, 2, half, width), F32),
             *[pltpu.VMEM((SUBS // 2 - 1, 2, half, width), F32)] * 3,
+            pltpu.VMEM((SUBS // 2 - 1, half, width), F32),
             pltpu.VMEM((n_users, width), BF16),
             pltpu.VMEM((half, width), BF16),
             pltpu.VMEM((n_users, width), F32),
@@ -396,6 +452,8 @@
             *[pltpu.VMEM(arg.shape, arg.dtype) for arg in args[4:]],
             pltpu.SemaphoreType.DMA((SUBS // 2, 4, 2, PARTS)),
             pltpu.SemaphoreType.DMA((SUBS // 2, 4, 2, PARTS)),
+            pltpu.SemaphoreType.DMA((SUBS // 2 - 1,)),
+            pltpu.SemaphoreType.DMA((SUBS // 2 - 1,)),
             pltpu.SemaphoreType.DMA((12,)),
             pltpu.SemaphoreType.DMA((6,)),
         ],

time: 107 us -> 99.3 us (0.928); the launches traced: 106 us -> 99.2 us
  Pallas kernels: 105 us -> 98.5 us
    pallas_call x1, Pallas kernels: 102 us -> 95.7 us  [per_device(): pl.pallas_call(functools.partial(kernel, n_blk), out_shape=(jax.ShapeDtyp...]
where the time goes in v5:
time: 99.3 us; the launch traced here: 99.2 us
  Pallas kernels  98.5 us (99%)
    pallas_call x1, Pallas kernels, per_device(): pl.pallas_call(functools.partial(kernel, n_blk), out_shape=(jax.ShapeDtyp...  95.7 us
    pallas_call x1, Pallas kernels, per_device(): pl.pallas_call(write_out, out_shape=[jax.ShapeDtypeStruct(x.shape, x.dtyp...  2.83 us

profile of v5, /device:TPU:1, one launch (start us, length us, event | category | flops | bytes accessed | tf_op | source)
XLA Modules:
  0.0 99.2 jit_solution(276786495445841148)
XLA Ops:
  0.6 95.7 %shard_map.129 = (f32[1024,256]{1,0:T(8,128)}, f32[1024,256]{1,0:T(8,128)}, f32[512,256]{1,0:T(8,128)}, f32[512,256]{1,0:T(8,128)}) custom-call(f32[1024,256]{1,0:T(8,128)} %users_in.1, f32[1024,256]{1,0:T(8,128)} %user_accum_in.1, f32[512,256]{1,0:T(8,128)} %items_in.1, f32[512,256]{1,0:T(8,128)} %item_accum_in.1, s32[6,16]{1,0:T(8,128)} %seen_user_in.1, ...), custom_call_target="tpu_custom_call" | custom-call | flops 4831838208 | bytes 12582912 | tf_op jit(solution)/shard_map/pallas_call | solution.py:428
  96.3 2.8 %shard_map.130 = (f32[1024,256]{1,0:T(8,128)}, f32[1024,256]{1,0:T(8,128)}, f32[512,256]{1,0:T(8,128)}, f32[512,256]{1,0:T(8,128)}) custom-call(f32[1024,256]{1,0:T(8,128)} %get-tuple-element.8.refs_0_, f32[1024,256]{1,0:T(8,128)} %get-tuple-element.9.refs_1_, f32[512,256]{1,0:T(8,128)} %get-tuple-element.10.refs_2_, f32[512,256]{1,0:T(8,128)} %get-tuple-element.11.refs_3_), custom_call_target="tpu_custom_call" | custom-call | bytes 6291456 | tf_op jit(solution)/shard_map/pallas_call | solution.py:467
